TPU v7x, 256 devices: a whole 4x4x8 slice. The times are simulated.
256 devices in a mesh: rows: 32 (over y_hi, z, core), cols: 8 (over x, y_lo).
Axes of the slice: x: 4, y: 4 (y_hi: 2, y_lo: 2; y = y_hi * 2 + y_lo), z: 8, core: 2. Of those that a mesh axis runs over, the one named last changes fastest.
Arguments:
- codes: int32 [512, 393216], P('cols', 'rows'), may hold values from 0 to 63
- labels: int32 [393216], P('rows'), may hold values 0 or 1
- base_margin: float32 [393216], P('rows'), may hold values from -6 to 6
- node_id: int32 [393216], P('rows'), may hold values from 0 to 15
- split_feature: int32 [256], replicated, may hold values from 0 to 511
- threshold: int32 [256], replicated, may hold values from 0 to 62
- leaf_value: float32 [256], replicated, may hold values from -6 to 6
Outputs:
- split_gains: float32 [16, 32768], P(None, ('cols', 'rows'))
- best_gain: float32 [16], replicated
All inputs are finite; a program needn't handle non-finite values. No bound on the sum of `labels` on one device may be relied on, other than what follows from the above.
Results may differ from a plain program's by a relative error of at most 0.0015.
Values may be sent and summed in bfloat16 or wider, within the bound.
A program may use at most 64 MiB of HBM per device.

v0:
```python
import jax
import jax.numpy as jnp
from jax import lax
from jax.sharding import PartitionSpec as P

BINS = 64
NODES = 16


reg_lambda = 1.0
block_rows = 512


def shards(codes, labels, base_margin, node_id, split_feature, threshold, leaf_value):
    local_feats, samples = codes.shape
    tree_slots = leaf_value.shape[0]
    tree_depth = tree_slots.bit_length() - 1
    bin_count = BINS
    node_count = NODES
    feature_ids = lax.axis_index("cols") * local_feats + lax.iota(jnp.int32, local_feats)
    selector = (split_feature[:, None] == feature_ids[None, :]).astype(jnp.bfloat16)
    partial_codes = jnp.dot(
        selector, codes.astype(jnp.bfloat16), preferred_element_type=jnp.float32
    )
    code_table = partial_codes.astype(jnp.bfloat16)
    node_index = jnp.ones((samples,), jnp.int32)
    for depth_level in range(tree_depth):
        first_node = 2**depth_level
        level_codes = code_table[first_node : 2 * first_node, :].astype(jnp.float32)
        chosen_mask = lax.iota(jnp.int32, first_node)[:, None] == (node_index - first_node)[None, :]
        chosen = jnp.sum(jnp.where(chosen_mask, level_codes, 0.0), axis=0)
        bound = jnp.sum(
            jnp.where(chosen_mask, threshold[first_node : 2 * first_node, None], 0), axis=0
        )
        chosen = lax.psum(chosen.astype(jnp.bfloat16), "cols").astype(jnp.float32)
        node_index = 2 * node_index + (chosen > bound.astype(jnp.float32)).astype(jnp.int32)
    leaf_mask = lax.iota(jnp.int32, tree_slots)[:, None] == (node_index - tree_slots)[None, :]
    leaf_weight = jnp.sum(jnp.where(leaf_mask, leaf_value[:, None], 0.0), axis=0)
    margin = base_margin + leaf_weight
    probability = jax.nn.sigmoid(margin)
    gradient = (probability - labels.astype(jnp.float32)).astype(jnp.bfloat16)
    hessian = (probability * (1.0 - probability)).astype(jnp.bfloat16)
    node_mask = lax.iota(jnp.int32, node_count)[:, None] == node_id[None, :]
    zero_value = jnp.zeros((), jnp.bfloat16)
    weights = jnp.concatenate(
        [
            jnp.where(node_mask, gradient[None, :], zero_value),
            jnp.where(node_mask, hessian[None, :], zero_value),
        ],
        axis=0,
    )
    bin_ids = lax.iota(jnp.int32, bin_count)

    def accumulate(block_step, histogram):
        row_start = block_step * block_rows
        code_rows = lax.dynamic_slice_in_dim(codes, row_start, block_rows, 1)
        weight_rows = lax.dynamic_slice_in_dim(weights, row_start, block_rows, 1)
        onehot = (code_rows[:, None, :] == bin_ids[None, :, None]).astype(jnp.bfloat16)
        onehot = onehot.reshape(local_feats * bin_count, block_rows)
        return histogram + lax.dot_general(
            weight_rows, onehot, (((1,), (1,)), ((), ())), preferred_element_type=jnp.float32
        )

    histogram = lax.fori_loop(
        0,
        samples // block_rows,
        accumulate,
        jnp.zeros((2 * node_count, local_feats * bin_count), jnp.float32),
    )
    owned_width = local_feats * bin_count // lax.axis_size("rows")
    summed_hist = lax.psum(histogram, "rows")
    owned = lax.dynamic_slice_in_dim(
        summed_hist, lax.axis_index("rows") * owned_width, owned_width, 1
    )
    hist_stats = owned.reshape(2, node_count, owned_width // bin_count, bin_count)
    left_sums = jnp.cumsum(hist_stats, axis=3)
    node_sums = left_sums[:, :, :, -1:]
    right_sums = node_sums - left_sums
    grad_left, hess_left = (left_sums[0], left_sums[1])
    grad_right, hess_right = (right_sums[0], right_sums[1])
    grad_node, hess_node = (node_sums[0], node_sums[1])
    split_score = 0.5 * (
        grad_left * grad_left / (hess_left + reg_lambda)
        + grad_right * grad_right / (hess_right + reg_lambda)
        - grad_node * grad_node / (hess_node + reg_lambda)
    )
    split_gains = split_score.reshape(node_count, owned_width)
    best_gain = lax.pmax(jnp.max(split_gains, axis=1), ("rows", "cols"))
    return (split_gains, best_gain)


def solution(mesh):
    return jax.shard_map(
        shards,
        mesh=mesh,
        in_specs=(P("cols", "rows"), P("rows"), P("rows"), P("rows"), P(), P(), P()),
        out_specs=(P(None, ("cols", "rows")), P()),
        check_vma=False,
    )
```

profile of v0, /device:TPU:1, one launch (start us, length us, event | category | flops | bytes accessed | tf_op | source)
XLA Modules:
  0.0 732.3 jit_solution(2688236902724501985)
XLA Ops:
  13.7 3.7 convolution_convert_fusion
  17.4 2.7 copy-done
  20.2 28.1 %psum.63 = bf16[12288]{0:T(1024)(128)(2,1)S(1)} all-reduce(bf16[12288]{0:T(1024)(128)(2,1)S(1)} %slice_reduce_fusion), channel_id=1, replica_groups=mesh['rows'=32,'cols'=8] {'cols'}, use_global_device_ids=true, to_apply=%region_0.1 | all-reduce | flops 12288 | bytes 49152 | tf_op jit(solution)/shard_map/psum | solution.py:35
  50.1 23.7 %psum.64 = bf16[12288]{0:T(1024)(128)(2,1)S(1)} all-reduce(bf16[12288]{0:T(1024)(128)(2,1)S(1)} %select_reduce_fusion.14), channel_id=1, replica_groups=mesh['rows'=32,'cols'=8] {'cols'}, use_global_device_ids=true, to_apply=%region_2.3 | all-reduce | flops 12288 | bytes 49152 | tf_op jit(solution)/shard_map/psum | solution.py:35
  75.2 24.1 %psum.65 = bf16[12288]{0:T(1024)(128)(2,1)S(1)} all-reduce(bf16[12288]{0:T(1024)(128)(2,1)S(1)} %select_reduce_fusion.12), channel_id=1, replica_groups=mesh['rows'=32,'cols'=8] {'cols'}, use_global_device_ids=true, to_apply=%region_5.6 | all-reduce | flops 12288 | bytes 49152 | tf_op jit(solution)/shard_map/psum | solution.py:35
  100.6 23.7 %psum.66 = bf16[12288]{0:T(1024)(128)(2,1)S(1)} all-reduce(bf16[12288]{0:T(1024)(128)(2,1)S(1)} %select_reduce_fusion.10), channel_id=1, replica_groups=mesh['rows'=32,'cols'=8] {'cols'}, use_global_device_ids=true, to_apply=%region_8.9 | all-reduce | flops 12288 | bytes 49152 | tf_op jit(solution)/shard_map/psum | solution.py:35
  125.8 23.8 %psum.67 = bf16[12288]{0:T(1024)(128)(2,1)S(1)} all-reduce(bf16[12288]{0:T(1024)(128)(2,1)S(1)} %select_reduce_fusion.8), channel_id=1, replica_groups=mesh['rows'=32,'cols'=8] {'cols'}, use_global_device_ids=true, to_apply=%region_11.12 | all-reduce | flops 12288 | bytes 49152 | tf_op jit(solution)/shard_map/psum | solution.py:35
  149.9 1.5 select_reduce_fusion.6
  151.4 24.0 %psum.68 = bf16[12288]{0:T(1024)(128)(2,1)S(1)} all-reduce(bf16[12288]{0:T(1024)(128)(2,1)S(1)} %select_reduce_fusion.6), channel_id=1, replica_groups=mesh['rows'=32,'cols'=8] {'cols'}, use_global_device_ids=true, to_apply=%region_14.15 | all-reduce | flops 12288 | bytes 49152 | tf_op jit(solution)/shard_map/psum | solution.py:35
  175.7 2.0 select_reduce_fusion.4
  177.7 23.9 %psum.69 = bf16[12288]{0:T(1024)(128)(2,1)S(1)} all-reduce(bf16[12288]{0:T(1024)(128)(2,1)S(1)} %select_reduce_fusion.4), channel_id=1, replica_groups=mesh['rows'=32,'cols'=8] {'cols'}, use_global_device_ids=true, to_apply=%region_17.18 | all-reduce | flops 12288 | bytes 49152 | tf_op jit(solution)/shard_map/psum | solution.py:35
  202.1 2.9 select_reduce_fusion.2
  205.0 24.0 %psum.70 = bf16[12288]{0:T(1024)(128)(2,1)S(1)} all-reduce(bf16[12288]{0:T(1024)(128)(2,1)S(1)} %select_reduce_fusion.2), channel_id=1, replica_groups=mesh['rows'=32,'cols'=8] {'cols'}, use_global_device_ids=true, to_apply=%region_20.21 | all-reduce | flops 12288 | bytes 49152 | tf_op jit(solution)/shard_map/psum | solution.py:35
  230.1 2.1 select_reduce_fusion
  232.4 89.8 %while.14 = (s32[]{:T(128)}, f32[32,4096]{1,0:T(8,128)S(1)}, bf16[32,12288]{1,0:T(8,128)(2,1)S(1)}, s32[64,12288]{1,0:T(8,128)}, s32[]{:T(128)}, /*index=5*/s32[]{:T(128)}, s32[]{:T(128)}, s32[]{:T(128)}) while((s32[]{:T(128)}, f32[32,4096]{1,0:T(8,128)S(1)}, bf16[32,12288]{1,0:T(8,128)(2,1)S(1)}, s32[64,12288]{1,0:T(8,128)}, ...), condition=%wide.region_24.25_spmd.clone, body=%wide.region_23.24_spmd.clone.sunk | while | flops 136577024 | bytes 5734549 | solution.py:64
  242.3 1.4 convolution_add_fusion.2
  249.8 1.4 convolution_add_fusion.2
  253.5 1.4 convolution_add_fusion.2
  257.3 1.4 convolution_add_fusion.2
  272.2 1.4 convolution_add_fusion.2
  290.9 1.4 convolution_add_fusion.2
  309.7 1.4 convolution_add_fusion.2
  323.1 321.4 %all-reduce.2.cloned.1.call-done = f32[32,4096]{1,0:T(8,128)} async-done(((f32[32,4096]{1,0:T(8,128)}), f32[32,4096]{1,0:T(8,128)}) %all-reduce.2.cloned.1.call-update) | async-done | bytes 524304 | tf_op jit(solution)/shard_map/psum | solution.py:71
  647.2 77.6 %pmax.7 = f32[16]{0:T(128)} all-reduce(f32[16]{0:T(128)S(1)} %get-tuple-element.122), channel_id=1, replica_groups=mesh['rows'=32,'cols'=8] {'rows','cols'}, use_global_device_ids=true, to_apply=%region_28.29 | all-reduce | flops 16 | bytes 128 | tf_op jit(solution)/shard_map/pmax | solution.py:88
  (173 shorter events, 97.4 us)
Async XLA Ops:
  7.2 637.4 %all-reduce.2.cloned.1.call-start = ((), (), s32[]{:S(2)}) async-start(), calls=%async_computation | async-start | bytes 1048576 | tf_op jit(solution)/shard_map/psum | solution.py:71
  17.4 2.7 copy-start
  151.3 78.8 %copy-start.5 = (f32[256]{0:T(256)S(1)}, f32[256]{0:T(256)}, u32[]{:S(2)}) copy-start(f32[256]{0:T(256)} %param.15) | copy-start | bytes 3076
  151.3 80.8 %copy-start.3 = (s32[12288]{0:T(1024)S(1)}, s32[12288]{0:T(1024)}, u32[]{:S(2)}) copy-start(s32[12288]{0:T(1024)} %param.10) | copy-start | bytes 147460
  151.4 80.8 %copy-start.4 = (f32[12288]{0:T(1024)S(1)}, f32[12288]{0:T(1024)}, u32[]{:S(2)}) copy-start(f32[12288]{0:T(1024)} %param.11) | copy-start | bytes 147460
  151.4 80.9 %copy-start.2 = (s32[12288]{0:T(1024)S(1)}, s32[12288]{0:T(1024)}, u32[]{:S(2)}) copy-start(s32[12288]{0:T(1024)} %param.12) | copy-start | bytes 147460
  322.3 0.8 copy-start.1
Sparse Core Ops, SparseCore 0:
  323.2 321.2 all-reduce.1
where the time goes:
time: 734 us; the launch traced here: 732 us
  waiting for transfers between devices  321 us (44%)
  blocking collectives  273 us (37%)
  other arithmetic  49.9 us (7%)
  matrix products  36.5 us (5%)
  local copies, waits for them, and re-layouts  35.3 us (5%)
  between operations  14.9 us (2%)
    psum x1, waiting for transfers between devices, shards(): summed_hist = lax.psum(histogram, 'rows')  321 us
    psum x8, blocking collectives, shards(): chosen = lax.psum(chosen.astype(jnp.bfloat16), 'cols').astype(jnp.float32)  195 us
    pmax x1, blocking collectives, shards(): best_gain = lax.pmax(jnp.max(split_gains, axis=1), ('rows', 'cols'))  77.6 us
    dot_general x24, matrix products, accumulate(): lax.dot_general(weight_rows, onehot, (((1,), (1,)), ((), ())), preferred_...  32.8 us
    eq x24, other arithmetic, accumulate(): code_rows[:, None, :] == bin_ids[None, :, None]  31.9 us
    dynamic_slice x24, local copies, waits for them, and re-layouts, accumulate(): code_rows = lax.dynamic_slice_in_dim(codes, row_start, block_rows, 1)  22.1 us
  transfers between devices with their start and end apart: 1, of which 1 were waited for; matrix products, arithmetic and copies ran while one was open for 0% of the time, Pallas kernels for 0%

commit v1 on v0

v1 whole, which is shorter than its diff:
```python
import functools

import jax
import jax.numpy as jnp
from jax import lax
from jax.experimental import pallas as pl
from jax.experimental.pallas import tpu as pltpu
from jax.sharding import PartitionSpec as P

BINS = 64
NODES = 16
SUB = 16
PIECES = 8
GROUP = 4
reg_lambda = 1.0
MESH = pl.DeviceIdType.MESH
F32, BF16, F8, I8 = jnp.float32, jnp.bfloat16, jnp.float8_e4m3fn, jnp.int8


def walk(bits):
    rows = lax.broadcasted_iota(jnp.int32, bits.shape, 0)
    slot = jnp.ones((1, bits.shape[1]), jnp.int32)
    for _ in range(4):
        bit = jnp.sum(jnp.where(rows == slot, bits, 0.0), axis=0, keepdims=True)
        slot = 2 * slot + bit.astype(jnp.int32)
    return slot


def pieces_of(value):
    scaled = value * 2048.0
    whole = jnp.floor(scaled + 0.5)
    rest = (scaled - whole) * 256.0
    digits = []
    for _ in range(5):
        upper = jnp.floor(whole * 0.25 + 0.5)
        digits.append(whole - 4.0 * upper)
        whole = upper
    digits.append(whole)
    wide = rest * 1048577.0
    top = wide - (wide - rest)
    return digits + [top, (rest - top) * 16.0]


PIECE_SCALES = [4.0**i / 2048.0 for i in range(6)] + [2.0**-19, 2.0**-23]


def kernel(
    cols, chips,
    codes_ref, labels_ref, base_ref, node_ref, sf_ref, thr_ref, sfp_ref, thrp_ref, leaf_ref,
    gains_ref, best_ref,
    aug, cs, tab, sA, rA, sB, rB, subs, ps, W, pair_s, pair_r, hs, hr, m1s, m1r, m2s, m2r,
    semA, semS, semB, semP, semX, semH, semM, semN,
):
    feats, samples = codes_ref.shape
    C = samples // cols
    me = lax.axis_index("cols")
    row = lax.axis_index("rows")
    chip, core = row // 2, lax.rem(row, 2)

    def col_of(k):
        return lax.rem(me + k, cols)

    def chip_of(k):
        return lax.rem(chip + k, chips)

    def chunk(c):
        return pl.ds(pl.multiple_of(c * C, C), C)

    barrier = pltpu.get_barrier_semaphore()

    def greet(r, c):
        pl.semaphore_signal(barrier, inc=1, device_id=(r, c), device_id_type=MESH)

    for k in range(1, cols):
        greet(row, col_of(k))
    for k in range(cols):
        greet(chip * 2 + 1 - core, col_of(k))
    for k in range(1, chips):
        greet(chip_of(k) * 2 + core, me)

    aug[0:feats, :] = codes_ref[...].astype(BF16)
    aug[feats:, :] = jnp.where(lax.broadcasted_iota(jnp.int32, (16, samples), 0) == 0, 1.0, 0.0).astype(BF16)
    for g in range(chips):
        cs[g] = codes_ref[GROUP * g : GROUP * (g + 1), :].astype(I8)

    ids = lax.broadcasted_iota(jnp.int32, (feats, 256), 0) + me * feats
    last = lax.broadcasted_iota(jnp.int32, (16, 256), 0) == 0

    def selector(features, bounds):
        one = jnp.where(features == ids, 1.0, 0.0)
        low = jnp.where(last, -bounds.astype(F32), 0.0)
        return jnp.concatenate([one, low], axis=0).T.astype(BF16)

    top = selector(sf_ref[...], thr_ref[...])[0:SUB]
    deep = selector(sfp_ref[...], thrp_ref[...])

    pl.semaphore_wait(barrier, (cols - 1) + cols + (chips - 1))

    def to_cols(src, dst, sem, k):
        return pltpu.make_async_remote_copy(
            src_ref=src, dst_ref=dst, send_sem=sem.at[0, k], recv_sem=sem.at[1, k],
            device_id=(row, col_of(k)), device_id_type=MESH,
        )

    def top_bits(c):
        t = jnp.dot(top, aug[:, chunk(c)], preferred_element_type=F32)
        return jnp.where(t > 0.0, 1.0, 0.0).astype(BF16)

    def stepA(k, _):
        sA[k] = top_bits(col_of(k))
        to_cols(sA.at[k], rA.at[k], semA, k).start()
        return 0

    lax.fori_loop(1, cols, stepA, 0)
    rA[0] = top_bits(me)

    def table(c, _):
        tab[:, chunk(c)] = jnp.dot(deep, aug[:, chunk(c)], preferred_element_type=F32).astype(BF16)
        return 0

    lax.fori_loop(0, cols, table, 0)

    def waits(src, dst, sem):
        def w(k, _):
            to_cols(src.at[k], dst.at[k], sem, k).wait_recv()
            return 0

        lax.fori_loop(1, cols, w, 0)

    def sends(src, dst, sem):
        def w(k, _):
            to_cols(src.at[k], dst.at[k], sem, k).wait_send()
            return 0

        lax.fori_loop(1, cols, w, 0)

    def total(ref):
        s = ref[0].astype(F32)
        for k in range(1, cols):
            s = s + ref[k].astype(F32)
        return s

    waits(sA, rA, semA)
    mine = walk(total(rA)) - SUB
    subs[0] = mine.astype(F32)

    def stepS(k, _):
        to_cols(subs.at[0], subs.at[k], semS, k).start()
        return 0

    lax.fori_loop(1, cols, stepS, 0)

    def deep_bits(c, sub):
        sub = jnp.broadcast_to(sub, (SUB, C)).astype(BF16)
        got = jnp.zeros((SUB, C), BF16)
        for t in range(16):
            got = got + jnp.where(sub == BF16(t), tab[t * SUB : (t + 1) * SUB, chunk(c)], BF16(0))
        return jnp.where(got.astype(F32) > 0.0, 1.0, 0.0).astype(BF16)

    def stepB(k, _):
        to_cols(subs.at[0], subs.at[k], semS, k).wait_recv()
        back = cols - k
        sB[back] = deep_bits(col_of(back), subs[k])
        to_cols(sB.at[back], rB.at[back], semB, back).start()
        return 0

    lax.fori_loop(1, cols, stepB, 0)
    rB[0] = deep_bits(me, subs[0])
    leaf = leaf_ref[...]
    high = leaf.astype(BF16).astype(F32)
    mid = (leaf - high).astype(BF16).astype(F32)
    low = leaf - high - mid
    r16 = lax.broadcasted_iota(jnp.int32, (16, 256), 0)
    leaves = jnp.where(r16 == 0, high, jnp.where(r16 == 1, mid, jnp.where(r16 == 2, low, 0.0))).astype(BF16)
    waits(sB, rB, semB)
    at = mine * 16 + walk(total(rB)) - SUB
    onehot = jnp.where(lax.broadcasted_iota(jnp.int32, (256, C), 0) == at, 1.0, 0.0).astype(BF16)
    parts = jnp.dot(leaves, onehot, preferred_element_type=F32)
    weight = parts[0:1] + parts[1:2] + parts[2:3]
    ps[0] = jax.nn.sigmoid(base_ref[me] + weight)

    def stepP(k, _):
        to_cols(ps.at[0], ps.at[k], semP, k).start()
        return 0

    lax.fori_loop(1, cols, stepP, 0)

    def weights(k, c):
        p = ps[k]
        gradient = (p - labels_ref[c].astype(F32)).astype(BF16).astype(F32)
        hessian = (p * (1.0 - p)).astype(BF16).astype(F32) * 4.0
        node = jnp.broadcast_to(node_ref[c], (NODES, C)) == lax.broadcasted_iota(jnp.int32, (NODES, C), 0)
        for i, (a, b) in enumerate(zip(pieces_of(gradient), pieces_of(hessian))):
            both = jnp.concatenate([jnp.where(node, a, 0.0), jnp.where(node, b, 0.0)], axis=0)
            W[i * 32 : (i + 1) * 32, chunk(c)] = both.astype(F8)

    weights(0, me)

    def stepW(k, _):
        to_cols(ps.at[0], ps.at[k], semP, k).wait_recv()
        weights(k, col_of(cols - k))
        return 0

    lax.fori_loop(1, cols, stepW, 0)

    def pair(k):
        return pltpu.make_async_remote_copy(
            src_ref=pair_s.at[k], dst_ref=pair_r.at[k], send_sem=semX.at[0, k], recv_sem=semX.at[1, k],
            device_id=(chip * 2 + 1 - core, me), device_id_type=MESH,
        )

    def share(k):
        return pltpu.make_async_remote_copy(
            src_ref=hs.at[k], dst_ref=hr.at[k], send_sem=semH.at[0, k], recv_sem=semH.at[1, k],
            device_id=(chip_of(k) * 2 + core, me), device_id_type=MESH,
        )

    halves = 2
    Kc = samples // halves
    bins = lax.broadcasted_iota(jnp.int32, (BINS, Kc), 0).astype(I8)

    def block(k):
        g = chip_of(k)
        acc = jnp.zeros((32 * PIECES, GROUP * BINS), F32)
        for s in range(halves):
            at = slice(s * Kc, (s + 1) * Kc)
            onehot = jnp.concatenate(
                [
                    jnp.where(jnp.broadcast_to(cs[g, f : f + 1, at], (BINS, Kc)) == bins, jnp.ones((), F8), jnp.zeros((), F8))
                    for f in range(GROUP)
                ],
                axis=0,
            )
            acc = acc + lax.dot_general(W[:, at], onehot, (((1,), (1,)), ((), ())), preferred_element_type=F32)
        out = acc[0:32] * PIECE_SCALES[0]
        for i in range(1, PIECES):
            out = out + acc[i * 32 : (i + 1) * 32] * PIECE_SCALES[i]
        out = jnp.concatenate([out[0:16], out[16:32] * 0.25], axis=0)
        left, right = out[:, 0:128], out[:, 128:256]
        first = core == 0
        hs[k] = jnp.where(first, left, right)
        pair_s[k] = jnp.where(first, right, left)
        pair(k).start()

    def merge(k):
        pair(k).wait_recv()
        hs[k] = hs[k] + pair_r[k]

    def stepH(i, _):
        block(i)

        @pl.when(i > 1)
        def _():
            merge(i - 1)
            share(i - 1).start()

        return 0

    lax.fori_loop(1, chips, stepH, 0)
    block(0)
    merge(chips - 1)
    share(chips - 1).start()
    merge(0)
    hist = hs[0]

    def stepR(k, h):
        share(k).wait_recv()
        return h + hr[k]

    hist = lax.fori_loop(1, chips, stepR, hist)

    i0 = lax.broadcasted_iota(jnp.int32, (128, 128), 0)
    i1 = lax.broadcasted_iota(jnp.int32, (128, 128), 1)
    same = (i0 // BINS) == (i1 // BINS)
    upto = jnp.where(same & (i0 <= i1), 1.0, 0.0)
    whole = jnp.where(same, 1.0, 0.0)
    left = jnp.dot(hist, upto, precision=lax.Precision.HIGHEST, preferred_element_type=F32)
    node = jnp.dot(hist, whole, precision=lax.Precision.HIGHEST, preferred_element_type=F32)
    right = node - left

    def score(s):
        return s[0:16] * s[0:16] / (s[16:32] + reg_lambda)

    gains = 0.5 * (score(left) + score(right) - score(node))
    gains_ref[...] = gains

    best = jnp.max(gains, axis=1, keepdims=True)
    d0 = lax.broadcasted_iota(jnp.int32, (16, 128), 0)
    d1 = lax.broadcasted_iota(jnp.int32, (16, 128), 1)
    best = jnp.max(jnp.where(d0 == d1, best, -jnp.inf), axis=0, keepdims=True)
    m1s[...] = best

    def first(k):
        return pltpu.make_async_remote_copy(
            src_ref=m1s, dst_ref=m1r.at[k], send_sem=semM.at[0, k], recv_sem=semM.at[1, k],
            device_id=(chip_of(k) * 2 + core, me), device_id_type=MESH,
        )

    def second(k):
        other, c = k // cols, lax.rem(k, cols)
        return pltpu.make_async_remote_copy(
            src_ref=m2s, dst_ref=m2r.at[k], send_sem=semN.at[0, k], recv_sem=semN.at[1, k],
            device_id=(chip * 2 + lax.rem(core + other, 2), col_of(c)), device_id_type=MESH,
        )

    def exchange(n, copy, got, best):
        def go(k, _):
            copy(k).start()
            return 0

        def take(k, b):
            copy(k).wait_recv()
            return jnp.maximum(b, got[k])

        lax.fori_loop(1, n, go, 0)
        return lax.fori_loop(1, n, take, best)

    best = exchange(chips, first, m1r, best)
    m2s[...] = best
    best = exchange(2 * cols, second, m2r, best)
    best_ref[...] = best[:, 0:16]

    sends(sA, rA, semA)
    sends(sB, rB, semB)

    def leftS(k, _):
        to_cols(subs.at[0], subs.at[k], semS, k).wait_send()
        to_cols(ps.at[0], ps.at[k], semP, k).wait_send()
        return 0

    lax.fori_loop(1, cols, leftS, 0)

    def leftX(k, _):
        pair(k).wait_send()
        return 0

    lax.fori_loop(0, chips, leftX, 0)

    def leftH(k, _):
        share(k).wait_send()
        first(k).wait_send()
        return 0

    lax.fori_loop(1, chips, leftH, 0)

    def leftN(k, _):
        second(k).wait_send()
        return 0

    lax.fori_loop(1, 2 * cols, leftN, 0)


def by_subtree(slots):
    parts = [slots[0:16].reshape(16, 1)]
    for level in range(4):
        n = 2**level
        parts.append(slots[16 * n : 32 * n].reshape(16, n))
    return jnp.concatenate(parts, axis=1).reshape(1, 256)


def shards(cols, rows, codes, labels, base_margin, node_id, split_feature, threshold, leaf_value):
    feats, samples = codes.shape
    chips = rows // 2
    C = samples // cols
    vm = pl.BlockSpec(memory_space=pltpu.VMEM)
    dma = pltpu.SemaphoreType.DMA
    by_col = lambda a: a.reshape(cols, 1, C)
    gains, best = pl.pallas_call(
        functools.partial(kernel, cols, chips),
        out_shape=(jax.ShapeDtypeStruct((NODES, 128), F32), jax.ShapeDtypeStruct((1, NODES), F32)),
        in_specs=[vm] * 9,
        out_specs=(vm, vm),
        scratch_shapes=[
            pltpu.VMEM((feats + 16, samples), BF16),
            pltpu.VMEM((chips, GROUP, samples), I8),
            pltpu.VMEM((256, samples), BF16),
            pltpu.VMEM((cols, SUB, C), BF16),
            pltpu.VMEM((cols, SUB, C), BF16),
            pltpu.VMEM((cols, SUB, C), BF16),
            pltpu.VMEM((cols, SUB, C), BF16),
            pltpu.VMEM((cols, 1, C), F32),
            pltpu.VMEM((cols, 1, C), F32),
            pltpu.VMEM((32 * PIECES, samples), F8),
            pltpu.VMEM((chips, 32, 128), F32),
            pltpu.VMEM((chips, 32, 128), F32),
            pltpu.VMEM((chips, 32, 128), F32),
            pltpu.VMEM((chips, 32, 128), F32),
            pltpu.VMEM((1, 128), F32),
            pltpu.VMEM((chips, 1, 128), F32),
            pltpu.VMEM((1, 128), F32),
            pltpu.VMEM((2 * cols, 1, 128), F32),
            dma((2, cols)),
            dma((2, cols)),
            dma((2, cols)),
            dma((2, cols)),
            dma((2, chips)),
            dma((2, chips)),
            dma((2, chips)),
            dma((2, 2 * cols)),
        ],
        compiler_params=pltpu.CompilerParams(
            collective_id=0, has_side_effects=True, vmem_limit_bytes=56 * 2**20
        ),
        cost_estimate=pl.CostEstimate(flops=2 * 256 * samples * feats * BINS, bytes_accessed=4 * feats * samples, transcendentals=samples),
    )(
        codes, by_col(labels), by_col(base_margin), by_col(node_id),
        split_feature.reshape(1, 256), threshold.reshape(1, 256),
        by_subtree(split_feature), by_subtree(threshold), leaf_value.reshape(1, 256),
    )
    return gains, best.reshape(NODES)


def solution(mesh):
    return jax.shard_map(
        functools.partial(shards, mesh.shape["cols"], mesh.shape["rows"]),
        mesh=mesh,
        in_specs=(P("cols", "rows"), P("rows"), P("rows"), P("rows"), P(), P(), P()),
        out_specs=(P(None, ("cols", "rows")), P()),
        check_vma=False,
    )
```

time: 734 us -> 80.6 us (0.11)
  waiting for transfers between devices: 321 us -> 0 us
  blocking collectives: 273 us -> 0 us
  Pallas kernels: 0 us -> 68.9 us
  other arithmetic: 49.9 us -> 0 us
  matrix products: 36.5 us -> 0 us
  local copies, waits for them, and re-layouts: 35.3 us -> 10.8 us
  between operations: 14.9 us -> 0.65 us
    psum x1 -> x0, waiting for transfers between devices: 321 us -> none  [shards(): summed_hist = lax.psum(histogram, 'rows')]
    psum x8 -> x0, blocking collectives: 195 us -> none  [shards(): chosen = lax.psum(chosen.astype(jnp.bfloat16), 'cols').astype(jnp.float32)]
    pmax x1 -> x0, blocking collectives: 77.6 us -> none  [shards(): best_gain = lax.pmax(jnp.max(split_gains, axis=1), ('rows', 'cols'))]
    pallas_call x0 -> x1, Pallas kernels: none -> 68.9 us  [shards(): pl.pallas_call(functools.partial(kernel, cols, chips), out_shape=(jax.Sha...]
    dot_general x25 -> x0, matrix products: 36.5 us -> none  [the longest x24 32.8 us: accumulate(): lax.dot_general(weight_rows, onehot, (((1,), (1,)), ((), ())), preferred_...]
    eq x24 -> x0, other arithmetic: 31.9 us -> none  [accumulate(): code_rows[:, None, :] == bin_ids[None, :, None]]
    dynamic_slice x25 -> x0, local copies, waits for them, and re-layouts: 22.8 us -> none  [the longest x24 22.1 us: accumulate(): code_rows = lax.dynamic_slice_in_dim(codes, row_start, block_rows, 1)]
    reduce_sum x15 -> x0, other arithmetic: 15.7 us -> none  [the longest x7 10.9 us: shards(): chosen = jnp.sum(jnp.where(chosen_mask, level_codes, 0.0), axis=0)]
  transfers between devices with their start and end apart: 1 -> 0, of which waited for: 1 -> 0; matrix products, arithmetic and copies ran while one was open for 0% -> 0% of each run, Pallas kernels for 0% -> 0%
where the time goes in v1:
time: 80.6 us; the launch traced here: 80.3 us
  Pallas kernels  68.9 us (85%)
  local copies, waits for them, and re-layouts  10.8 us (13%)
    pallas_call x1, Pallas kernels, shards(): pl.pallas_call(functools.partial(kernel, cols, chips), out_shape=(jax.Sha...  68.9 us
    slice x8, local copies, waits for them, and re-layouts, by_subtree(): parts.append(slots[16 * n:32 * n].reshape(16, n))  4.57 us
    unnamed x2, local copies, waits for them, and re-layouts  2.41 us
    reshape x8, local copies, waits for them, and re-layouts, by_subtree(): parts.append(slots[16 * n:32 * n].reshape(16, n))  2.14 us

profile of v1, /device:TPU:1, one launch (start us, length us, event | category | flops | bytes accessed | tf_op | source)
XLA Modules:
  0.0 80.3 jit_solution(12549332486885475578)
XLA Ops:
  0.6 0.8 %slice_bitcast_fusion = (s32[16,1]{0,1:T(1,128)S(1)}, s32[16,1]{0,1:T(1,128)S(1)}) fusion(s32[256]{0:T(256)} %param.12), kind=kLoop, calls=%fused_computation | loop fusion | bytes 256 | tf_op jit(solution)/shard_map/reshape | solution.py:357
  1.5 0.1 copy.15
  1.5 0.1 copy.16
  1.6 0.7 slice.92
  2.4 0.1 reshape.117
  2.5 0.7 slice.93
  3.1 0.1 reshape.118
  3.2 0.8 slice.90
  4.0 0.1 slice.91
  4.1 0.1 concatenate.7
  4.2 0.6 reshape.119.thrp_ref
  4.8 0.8 %slice_bitcast_fusion.2 = (s32[16,1]{0,1:T(1,128)S(1)}, s32[16,1]{0,1:T(1,128)S(1)}) fusion(s32[256]{0:T(256)} %param.11), kind=kLoop, calls=%fused_computation.2 | loop fusion | bytes 256 | tf_op jit(solution)/shard_map/reshape | solution.py:357
  5.6 0.1 copy.13
  5.7 0.1 copy.14
  5.8 0.7 slice.86
  6.5 0.1 reshape.112
  6.6 0.7 slice.87
  7.3 0.1 reshape.113
  7.4 0.8 slice.84
  8.2 0.1 concatenate.6
  8.3 0.7 reshape.114.sfp_ref
  9.0 68.9 %shard_map.86 = (f32[16,128]{1,0:T(8,128)}, f32[1,16]{1,0:T(1,128)}) custom-call(s32[64,12288]{1,0:T(8,128)} %codes_ref.1, s32[8,1,1536]{2,1,0:T(1,128)} %bitcast.17, f32[8,1,1536]{2,1,0:T(1,128)} %bitcast.18, s32[8,1,1536]{2,1,0:T(1,128)} %bitcast.19, s32[1,256]{1,0:T(1,128)} %bitcast.15, s32[1,256]{1,0:T(1,128)} %bitcast.16, s32[1,256]{1,0:T(1,128)} %reshape.114.sfp_ref, ...), custom_call_target="tpu_custom_call" | custom-call | flops 25769803776 | bytes 3145728 | tf_op jit(solution)/shard_map/pallas_call | solution.py:368
  77.9 1.3 %copy.19 = f32[16,128]{1,0:T(8,128)} copy(f32[16,128]{1,0:T(8,128)} %get-tuple-element.12) | data formatting | bytes 16384
  79.2 1.1 %copy.20 = f32[16]{0:T(128)} copy(f32[16]{0:T(128)} %bitcast.21) | data formatting | bytes 128
  (1 shorter events, 0.1 us)

commit v2 on v0

v2 whole, which is shorter than its diff:
```python
import functools

import jax
import jax.numpy as jnp
from jax import lax
from jax.experimental import pallas as pl
from jax.experimental.pallas import tpu as pltpu
from jax.sharding import PartitionSpec as P

BINS = 64
NODES = 16
SUB = 16
PIECES = 8
GROUP = 4
PARTS = 2
reg_lambda = 1.0
MESH = pl.DeviceIdType.MESH
F32, BF16, F8, I8 = jnp.float32, jnp.bfloat16, jnp.float8_e4m3fn, jnp.int8
PIECE_SCALES = [4.0**i / 2048.0 for i in range(6)] + [2.0**-19, 2.0**-23]


def walk(bits):
    rows = lax.broadcasted_iota(jnp.int32, bits.shape, 0)
    slot = jnp.ones((1, bits.shape[1]), jnp.int32)
    for _ in range(4):
        bit = jnp.sum(jnp.where(rows == slot, bits, 0.0), axis=0, keepdims=True)
        slot = 2 * slot + bit.astype(jnp.int32)
    return slot


def pieces_of(value):
    scaled = value * 2048.0
    whole = jnp.floor(scaled + 0.5)
    rest = (scaled - whole) * 256.0
    digits = []
    for _ in range(5):
        upper = jnp.floor(whole * 0.25 + 0.5)
        digits.append(whole - 4.0 * upper)
        whole = upper
    digits.append(whole)
    wide = rest * 1048577.0
    top = wide - (wide - rest)
    return digits + [top, (rest - top) * 16.0]


def wait_bytes(ref, sem):
    pltpu.make_async_copy(ref, ref, sem).wait()


def kernel(
    cols, chips,
    codes_in, labels_in, base_in, node_in, sf_in, thr_in, leaf_in,
    out_ref,
    codes_ref, labels_ref, base_ref, node_ref, sf_ref, thr_ref, leaf_ref, sums,
    aug, cs, tab, sA, rA, sB, rB, subs, ps, W, pair_s, pair_r, hs, hr, m1s, m1r, m2s, m2r,
    semA, semS, semB, semP, sentS, sentP, semX, sentX, semH, semM, semN, semC, semI,
):
    feats, samples = codes_ref.shape
    Kc = samples // PARTS
    C = Kc // cols
    me = lax.axis_index("cols")
    row = lax.axis_index("rows")
    chip, core = row // 2, lax.rem(row, 2)
    planes = 2
    ring = chips // planes
    plane, place = chip // ring, lax.rem(chip, ring)

    def col_of(k):
        return lax.rem(me + k, cols)

    def chunk(q, c):
        return pl.ds(pl.multiple_of((q * cols + c) * C, C), C)

    barrier = pltpu.get_barrier_semaphore()

    def greet(r, c):
        pl.semaphore_signal(barrier, inc=1, device_id=(r, c), device_id_type=MESH)

    for k in range(1, chips):
        greet(lax.rem(chip + k, chips) * 2 + core, me)
    for k in range(1, cols):
        greet(row, col_of(k))
    for k in range(cols):
        greet(chip * 2 + 1 - core, col_of(k))

    small = [
        pltpu.make_async_copy(a, b, semI.at[n])
        for n, (a, b) in enumerate(
            [(sf_in, sf_ref), (thr_in, thr_ref), (leaf_in, leaf_ref), (base_in, base_ref), (labels_in, labels_ref), (node_in, node_ref)]
        )
    ]
    big = []
    for q in range(PARTS):
        at = pl.ds(q * Kc, Kc)
        big.append(pltpu.make_async_copy(codes_in.at[:, at], codes_ref.at[:, at], semC.at[q]))
    for copy in small[:2] + big + small[2:]:
        copy.start()

    i0 = lax.broadcasted_iota(jnp.int32, (128, 256), 0)
    i1 = lax.broadcasted_iota(jnp.int32, (128, 256), 1)
    same = (i0 // BINS) == ((i1 % 128) // BINS)
    sums[...] = jnp.where(same & ((i0 <= i1) | (i1 >= 128)), 1.0, 0.0)

    aug[feats:, :] = jnp.where(lax.broadcasted_iota(jnp.int32, (16, samples), 0) == 0, 1.0, 0.0).astype(BF16)

    for copy in small[:2]:
        copy.wait()

    ids = lax.broadcasted_iota(jnp.int32, (feats, 256), 0) + me * feats
    low = lax.broadcasted_iota(jnp.int32, (16, 256), 0) == 0
    picks = jnp.concatenate(
        [jnp.where(sf_ref[...] == ids, 1.0, 0.0), jnp.where(low, -thr_ref[...].astype(F32), 0.0)], axis=0
    ).astype(BF16)

    def rows_of(slots):
        order = jnp.where(slots == lax.broadcasted_iota(jnp.int32, slots.shape, 1), 1.0, 0.0).astype(BF16)
        return lax.dot_general(order, picks, (((1,), (1,)), ((), ())), preferred_element_type=F32).astype(BF16)

    top = rows_of(lax.broadcasted_iota(jnp.int32, (SUB, 256), 0))

    for q in range(PARTS):
        at = slice(q * Kc, (q + 1) * Kc)
        big[q].wait()
        aug[0:feats, at] = codes_ref[:, at].astype(BF16)

    pl.semaphore_wait(barrier, (cols - 1) + cols + (chips - 1))

    def to_col(src, dst, sent, came, k):
        return pltpu.make_async_remote_copy(
            src_ref=src, dst_ref=dst, send_sem=sent, recv_sem=came, device_id=(row, col_of(k)), device_id_type=MESH
        )

    others = pl.ds(1, cols - 1)

    def top_bits(q, c):
        t = jnp.dot(top, aug[:, chunk(q, c)], preferred_element_type=F32)
        return jnp.where(t > 0.0, 1.0, 0.0).astype(BF16)

    for q in range(PARTS):
        for k in range(1, cols):
            sA[q, k] = top_bits(q, col_of(k))
            to_col(sA.at[q, k], rA.at[q, k], semA.at[0, q], semA.at[1, q], k).start()
        rA[q, 0] = top_bits(q, me)

    at = lax.broadcasted_iota(jnp.int32, (256, 256), 0)
    t, r = at // SUB, at % SUB
    width = jnp.where(r >= 8, 8, jnp.where(r >= 4, 4, jnp.where(r >= 2, 2, 1)))
    deep = rows_of((16 + t) * width + r - width)

    def table(n, _):
        where = pl.ds(pl.multiple_of(n * C, C), C)
        tab[:, where] = jnp.dot(deep, aug[:, where], preferred_element_type=F32).astype(BF16)
        return 0

    lax.fori_loop(0, PARTS * cols, table, 0)

    def total(ref, q):
        s = ref[q, 0].astype(F32)
        for k in range(1, cols):
            s = s + ref[q, k].astype(F32)
        return s

    mine = []
    for q in range(PARTS):
        wait_bytes(rA.at[q, others], semA.at[1, q])
        mine.append(walk(total(rA, q)) - SUB)
        subs[q, 0] = mine[q].astype(F32)
        for k in range(1, cols):
            to_col(subs.at[q, 0], subs.at[q, k], sentS.at[q], semS.at[q, k], k).start()

    def deep_bits(q, c, sub):
        sub = jnp.broadcast_to(sub, (SUB, C)).astype(BF16)
        got = jnp.zeros((SUB, C), BF16)
        for t in range(16):
            got = got + jnp.where(sub == BF16(t), tab[t * SUB : (t + 1) * SUB, chunk(q, c)], BF16(0))
        return jnp.where(got.astype(F32) > 0.0, 1.0, 0.0).astype(BF16)

    for q in range(PARTS):
        rB[q, 0] = deep_bits(q, me, mine[q].astype(F32))

        def stepB(k, _):
            wait_bytes(subs.at[q, k], semS.at[q, k])
            back = cols - k
            sB[q, back] = deep_bits(q, col_of(back), subs[q, k])
            to_col(sB.at[q, back], rB.at[q, back], semB.at[0, q], semB.at[1, q], back).start()
            return 0

        lax.fori_loop(1, cols, stepB, 0)

    for copy in small[2:]:
        copy.wait()
    leaf = leaf_ref[...]
    high = leaf.astype(BF16).astype(F32)
    mid = (leaf - high).astype(BF16).astype(F32)
    rest = leaf - high - mid
    r16 = lax.broadcasted_iota(jnp.int32, (16, 256), 0)
    leaves = jnp.where(r16 == 0, high, jnp.where(r16 == 1, mid, jnp.where(r16 == 2, rest, 0.0))).astype(BF16)

    v8 = codes_ref[...].astype(I8)
    for g in range(chips):
        cs[g] = v8[GROUP * g : GROUP * (g + 1)]

    for q in range(PARTS):
        wait_bytes(rB.at[q, others], semB.at[1, q])
        slot = mine[q] * 16 + walk(total(rB, q)) - SUB
        onehot = jnp.where(lax.broadcasted_iota(jnp.int32, (256, C), 0) == slot, 1.0, 0.0).astype(BF16)
        parts = jnp.dot(leaves, onehot, preferred_element_type=F32)
        weight = parts[0:1] + parts[1:2] + parts[2:3]
        ps[q, 0] = jax.nn.sigmoid(base_ref[q * cols + me] + weight)
        for k in range(1, cols):
            to_col(ps.at[q, 0], ps.at[q, k], sentP.at[q], semP.at[q, k], k).start()

    def weights(q, k, c):
        p = ps[q, k]
        n = q * cols + c
        gradient = (p - labels_ref[n].astype(F32)).astype(BF16).astype(F32)
        hessian = (p * (1.0 - p)).astype(BF16).astype(F32) * 4.0
        here = jnp.broadcast_to(node_ref[n].astype(F32), (NODES, C)).astype(BF16)
        node = here == lax.broadcasted_iota(jnp.int32, (NODES, C), 0).astype(F32).astype(BF16)
        for i, v in enumerate(pieces_of(jnp.concatenate([gradient, hessian], axis=0))):
            a = jnp.broadcast_to(v[0:1], (NODES, C)).astype(BF16)
            b = jnp.broadcast_to(v[1:2], (NODES, C)).astype(BF16)
            both = jnp.concatenate([jnp.where(node, a, BF16(0)), jnp.where(node, b, BF16(0))], axis=0)
            W[i * 32 : (i + 1) * 32, chunk(q, c)] = both.astype(F8)

    def all_weights(q):
        weights(q, 0, me)

        def stepW(k, _):
            wait_bytes(ps.at[q, k], semP.at[q, k])
            weights(q, k, col_of(cols - k))
            return 0

        lax.fori_loop(1, cols, stepW, 0)

    def chip_of(i):
        j, far = lax.rem(i, ring), 1 - i // ring
        odd = lax.rem(j, 2)
        dz = odd * (ring // 2 - (j + 1) // 2) + (1 - odd) * (ring // 2 + j // 2)
        return lax.rem(plane + far, planes) * ring + lax.rem(place + dz, ring)

    def pair(i):
        return pltpu.make_async_remote_copy(
            src_ref=pair_s.at[i], dst_ref=pair_r.at[i], send_sem=sentX.at[0], recv_sem=semX.at[i],
            device_id=(chip * 2 + 1 - core, me), device_id_type=MESH,
        )

    def share(i):
        return pltpu.make_async_remote_copy(
            src_ref=hs.at[i], dst_ref=hr.at[i], send_sem=semH.at[0], recv_sem=semH.at[1],
            device_id=(chip_of(i) * 2 + core, me), device_id_type=MESH,
        )

    for q in range(PARTS):
        all_weights(q)

    bins = lax.broadcasted_iota(jnp.int32, (BINS, samples), 0).astype(I8)

    def block(i):
        g = chip_of(i)
        onehot = jnp.concatenate(
            [
                jnp.where(
                    jnp.broadcast_to(cs[g, f : f + 1, :], (BINS, samples)) == bins, jnp.ones((), F8), jnp.zeros((), F8)
                )
                for f in range(GROUP)
            ],
            axis=0,
        )
        acc = lax.dot_general(W[...], onehot, (((1,), (1,)), ((), ())), preferred_element_type=F32)
        out = acc[0:32] * PIECE_SCALES[0]
        for n in range(1, PIECES):
            out = out + acc[n * 32 : (n + 1) * 32] * PIECE_SCALES[n]
        out = jnp.concatenate([out[0:16], out[16:32] * 0.25], axis=0)
        left, right = out[:, 0:128], out[:, 128:256]
        first = core == 0
        hs[i] = jnp.where(first, left, right)
        pair_s[i] = jnp.where(first, right, left)
        pair(i).start()

    def merge(i):
        wait_bytes(pair_r.at[i], semX.at[i])
        hs[i] = hs[i] + pair_r[i]

    def stepH(n, _):
        block(2 * n)

        @pl.when(n > 0)
        def _():
            merge(2 * n - 1)
            share(2 * n - 1).start()

        block(2 * n + 1)
        merge(2 * n)
        share(2 * n).start()
        return 0

    lax.fori_loop(0, chips // 2, stepH, 0)
    merge(chips - 1)
    wait_bytes(hr.at[pl.ds(0, chips - 1)], semH.at[1])
    hist = hs[chips - 1]
    for i in range(chips - 1):
        hist = hist + hr[i]

    both = jnp.dot(hist, sums[...], precision=lax.Precision.HIGHEST, preferred_element_type=F32)
    left, node = both[:, 0:128], both[:, 128:256]
    right = node - left

    def score(s):
        return s[0:16] * s[0:16] / (s[16:32] + reg_lambda)

    gains = 0.5 * (score(left) + score(right) - score(node))
    out_ref[0:NODES, :] = gains

    best = jnp.max(gains, axis=1, keepdims=True)
    d0 = lax.broadcasted_iota(jnp.int32, (16, 128), 0)
    d1 = lax.broadcasted_iota(jnp.int32, (16, 128), 1)
    best = jnp.max(jnp.where(d0 == d1, best, -jnp.inf), axis=0, keepdims=True)

    def exchange(n, src, got, sem, device, best):
        src[...] = best
        for k in range(1, n):
            pltpu.make_async_remote_copy(
                src_ref=src, dst_ref=got.at[k], send_sem=sem.at[0], recv_sem=sem.at[1],
                device_id=device(k), device_id_type=MESH,
            ).start()
        wait_bytes(got.at[pl.ds(1, n - 1)], sem.at[1])
        for k in range(1, n):
            best = jnp.maximum(best, got[k])
        return best

    best = exchange(chips, m1s, m1r, semM, lambda k: (lax.rem(chip + k, chips) * 2 + core, me), best)
    best = exchange(
        2 * cols, m2s, m2r, semN, lambda k: (chip * 2 + lax.rem(core + k // cols, 2), col_of(k % cols)), best
    )
    out_ref[NODES:, :] = jnp.broadcast_to(best, (8, 128))

    for q in range(PARTS):
        wait_bytes(sA.at[q, others], semA.at[0, q])
        wait_bytes(sB.at[q, others], semB.at[0, q])
        wait_bytes(subs.at[q, others], sentS.at[q])
        wait_bytes(ps.at[q, others], sentP.at[q])
    wait_bytes(pair_s, sentX.at[0])
    wait_bytes(hs.at[pl.ds(0, chips - 1)], semH.at[0])
    wait_bytes(m1r.at[pl.ds(1, chips - 1)], semM.at[0])
    wait_bytes(m2r.at[pl.ds(1, 2 * cols - 1)], semN.at[0])


def shards(cols, rows, codes, labels, base_margin, node_id, split_feature, threshold, leaf_value):
    feats, samples = codes.shape
    chips = rows // 2
    C = samples // (cols * PARTS)
    vm = pl.BlockSpec(memory_space=pltpu.VMEM)
    anywhere = pl.BlockSpec(memory_space=pl.ANY)
    I32 = jnp.int32
    dma = pltpu.SemaphoreType.DMA
    by_chunk = lambda a: a.reshape(cols * PARTS, 1, C)
    out = pl.pallas_call(
        functools.partial(kernel, cols, chips),
        out_shape=jax.ShapeDtypeStruct((NODES + 8, 128), F32),
        in_specs=[anywhere] * 7,
        out_specs=vm,
        scratch_shapes=[
            pltpu.VMEM((feats, samples), I32),
            pltpu.VMEM((cols * PARTS, 1, C), I32),
            pltpu.VMEM((cols * PARTS, 1, C), F32),
            pltpu.VMEM((cols * PARTS, 1, C), I32),
            pltpu.VMEM((1, 256), I32),
            pltpu.VMEM((1, 256), I32),
            pltpu.VMEM((1, 256), F32),
            pltpu.VMEM((128, 256), F32),
            pltpu.VMEM((feats + 16, samples), BF16),
            pltpu.VMEM((chips, GROUP, samples), I8),
            pltpu.VMEM((256, samples), BF16),
            pltpu.VMEM((PARTS, cols, SUB, C), BF16),
            pltpu.VMEM((PARTS, cols, SUB, C), BF16),
            pltpu.VMEM((PARTS, cols, SUB, C), BF16),
            pltpu.VMEM((PARTS, cols, SUB, C), BF16),
            pltpu.VMEM((PARTS, cols, 1, C), F32),
            pltpu.VMEM((PARTS, cols, 1, C), F32),
            pltpu.VMEM((32 * PIECES, samples), F8),
            pltpu.VMEM((chips, 32, 128), F32),
            pltpu.VMEM((chips, 32, 128), F32),
            pltpu.VMEM((chips, 32, 128), F32),
            pltpu.VMEM((chips, 32, 128), F32),
            pltpu.VMEM((1, 128), F32),
            pltpu.VMEM((chips, 1, 128), F32),
            pltpu.VMEM((1, 128), F32),
            pltpu.VMEM((2 * cols, 1, 128), F32),
            dma((2, PARTS)),
            dma((PARTS, cols)),
            dma((2, PARTS)),
            dma((PARTS, cols)),
            dma((PARTS,)),
            dma((PARTS,)),
            dma((chips,)),
            dma((1,)),
            dma((2,)),
            dma((2,)),
            dma((2,)),
            dma((PARTS,)),
            dma((6,)),
        ],
        compiler_params=pltpu.CompilerParams(
            collective_id=0, has_side_effects=True, vmem_limit_bytes=56 * 2**20
        ),
        cost_estimate=pl.CostEstimate(
            flops=2 * 256 * samples * feats * BINS, bytes_accessed=4 * feats * samples, transcendentals=samples
        ),
    )(
        codes, by_chunk(labels), by_chunk(base_margin), by_chunk(node_id),
        split_feature.reshape(1, 256), threshold.reshape(1, 256), leaf_value.reshape(1, 256),
    )
    return out[0:NODES], out[NODES, 0:NODES]


def solution(mesh):
    return jax.shard_map(
        functools.partial(shards, mesh.shape["cols"], mesh.shape["rows"]),
        mesh=mesh,
        in_specs=(P("cols", "rows"), P("rows"), P("rows"), P("rows"), P(), P(), P()),
        out_specs=(P(None, ("cols", "rows")), P()),
        check_vma=False,
    )
```

time: 734 us -> 77.3 us (0.11)
  waiting for transfers between devices: 321 us -> 0 us
  blocking collectives: 273 us -> 0 us
  Pallas kernels: 0 us -> 74 us
  other arithmetic: 49.9 us -> 0 us
  matrix products: 36.5 us -> 0 us
  local copies, waits for them, and re-layouts: 35.3 us -> 2.48 us
  between operations: 14.9 us -> 0.64 us
    psum x1 -> x0, waiting for transfers between devices: 321 us -> none  [shards(): summed_hist = lax.psum(histogram, 'rows')]
    psum x8 -> x0, blocking collectives: 195 us -> none  [shards(): chosen = lax.psum(chosen.astype(jnp.bfloat16), 'cols').astype(jnp.float32)]
    pmax x1 -> x0, blocking collectives: 77.6 us -> none  [shards(): best_gain = lax.pmax(jnp.max(split_gains, axis=1), ('rows', 'cols'))]
    pallas_call x0 -> x1, Pallas kernels: none -> 74 us  [shards(): pl.pallas_call(functools.partial(kernel, cols, chips), out_shape=jax.Shap...]
    dot_general x25 -> x0, matrix products: 36.5 us -> none  [the longest x24 32.8 us: accumulate(): lax.dot_general(weight_rows, onehot, (((1,), (1,)), ((), ())), preferred_...]
    eq x24 -> x0, other arithmetic: 31.9 us -> none  [accumulate(): code_rows[:, None, :] == bin_ids[None, :, None]]
    dynamic_slice x25 -> x0, local copies, waits for them, and re-layouts: 22.8 us -> none  [the longest x24 22.1 us: accumulate(): code_rows = lax.dynamic_slice_in_dim(codes, row_start, block_rows, 1)]
    reduce_sum x15 -> x0, other arithmetic: 15.7 us -> none  [the longest x7 10.9 us: shards(): chosen = jnp.sum(jnp.where(chosen_mask, level_codes, 0.0), axis=0)]
  transfers between devices with their start and end apart: 1 -> 0, of which waited for: 1 -> 0; matrix products, arithmetic and copies ran while one was open for 0% -> 0% of each run, Pallas kernels for 0% -> 0%
where the time goes in v2:
time: 77.3 us; the launch traced here: 77.1 us
  Pallas kernels  74 us (96%)
  local copies, waits for them, and re-layouts  2.48 us (3%)
    pallas_call x1, Pallas kernels, shards(): pl.pallas_call(functools.partial(kernel, cols, chips), out_shape=jax.Shap...  74 us

profile of v2, /device:TPU:1, one launch (start us, length us, event | category | flops | bytes accessed | tf_op | source)
XLA Modules:
  0.0 77.1 jit_solution(7896289404356790425)
XLA Ops:
  0.6 74.0 %shard_map.86 = f32[24,128]{1,0:T(8,128)} custom-call(s32[64,12288]{1,0:T(8,128)} %codes_in.1, s32[16,1,768]{2,1,0:T(1,128)} %bitcast.8, f32[16,1,768]{2,1,0:T(1,128)} %bitcast.9, s32[16,1,768]{2,1,0:T(1,128)} %bitcast.10, s32[1,256]{1,0:T(1,128)} %bitcast.11, s32[1,256]{1,0:T(1,128)} %bitcast.12, f32[1,256]{1,0:T(1,128)} %bitcast.13), custom_call_target="tpu_custom_call" | custom-call | flops 25769803776 | bytes 3145728 | tf_op jit(solution)/shard_map/pallas_call | solution.py:358
  74.6 1.2 %slice_bitcast_fusion = f32[16]{0:T(128)} fusion(f32[24,128]{1,0:T(8,128)} %shard_map.86), kind=kLoop, calls=%fused_computation | loop fusion | bytes 128 | tf_op jit(solution)/shard_map/squeeze | solution.py:414
  75.8 1.3 %slice.6 = f32[16,128]{1,0:T(8,128)} slice(f32[24,128]{1,0:T(8,128)} %shard_map.86), slice={[0:16], [0:128]} | slice | bytes 16384 | tf_op jit(solution)/shard_map/slice | solution.py:414

commit v3 on v2

--- a/solution.py
+++ b/solution.py
@@ -282,20 +282,17 @@
         wait_bytes(pair_r.at[i], semX.at[i])
         hs[i] = hs[i] + pair_r[i]
 
-    def stepH(n, _):
-        block(2 * n)
-
-        @pl.when(n > 0)
+    def stepH(i, _):
+        block(i)
+
+        @pl.when(i > 0)
         def _():
-            merge(2 * n - 1)
-            share(2 * n - 1).start()
-
-        block(2 * n + 1)
-        merge(2 * n)
-        share(2 * n).start()
+            merge(i - 1)
+            share(i - 1).start()
+
         return 0
 
-    lax.fori_loop(0, chips // 2, stepH, 0)
+    lax.fori_loop(0, chips, stepH, 0)
     merge(chips - 1)
     wait_bytes(hr.at[pl.ds(0, chips - 1)], semH.at[1])
     hist = hs[chips - 1]

time: 77.3 us -> 64.6 us (0.84)
  Pallas kernels: 74 us -> 61.3 us
    pallas_call x1, Pallas kernels: 74 us -> 61.3 us  [shards(): pl.pallas_call(functools.partial(kernel, cols, chips), out_shape=jax.Shap...]
where the time goes in v3:
time: 64.6 us; the launch traced here: 64.4 us
  Pallas kernels  61.3 us (95%)
  local copies, waits for them, and re-layouts  2.48 us (4%)
    pallas_call x1, Pallas kernels, shards(): pl.pallas_call(functools.partial(kernel, cols, chips), out_shape=jax.Shap...  61.3 us
    slice x1, local copies, waits for them, and re-layouts, shards(): return (out[0:NODES], out[NODES, 0:NODES])  1.29 us

profile of v3, /device:TPU:1, one launch (start us, length us, event | category | flops | bytes accessed | tf_op | source)
XLA Modules:
  0.0 64.4 jit_solution(17514901830247794188)
XLA Ops:
  0.6 61.3 %shard_map.86 = f32[24,128]{1,0:T(8,128)} custom-call(s32[64,12288]{1,0:T(8,128)} %codes_in.1, s32[16,1,768]{2,1,0:T(1,128)} %bitcast.8, f32[16,1,768]{2,1,0:T(1,128)} %bitcast.9, s32[16,1,768]{2,1,0:T(1,128)} %bitcast.10, s32[1,256]{1,0:T(1,128)} %bitcast.11, s32[1,256]{1,0:T(1,128)} %bitcast.12, f32[1,256]{1,0:T(1,128)} %bitcast.13), custom_call_target="tpu_custom_call" | custom-call | flops 25769803776 | bytes 3145728 | tf_op jit(solution)/shard_map/pallas_call | solution.py:355
  61.9 1.2 %slice_bitcast_fusion = f32[16]{0:T(128)} fusion(f32[24,128]{1,0:T(8,128)} %shard_map.86), kind=kLoop, calls=%fused_computation | loop fusion | bytes 128 | tf_op jit(solution)/shard_map/squeeze | solution.py:411
  63.1 1.3 %slice.6 = f32[16,128]{1,0:T(8,128)} slice(f32[24,128]{1,0:T(8,128)} %shard_map.86), slice={[0:16], [0:128]} | slice | bytes 16384 | tf_op jit(solution)/shard_map/slice | solution.py:411

commit v4 on v2

--- a/solution.py
+++ b/solution.py
@@ -68,6 +68,10 @@
     def col_of(k):
         return lax.rem(me + k, cols)
 
+    def at_row(planes_on, places_on, cores_on):
+        there = lax.rem(plane + planes_on, planes) * ring + lax.rem(place + places_on, ring)
+        return there * 2 + lax.rem(core + cores_on, 2)
+
     def chunk(q, c):
         return pl.ds(pl.multiple_of((q * cols + c) * C, C), C)
 
@@ -80,8 +84,9 @@
         greet(lax.rem(chip + k, chips) * 2 + core, me)
     for k in range(1, cols):
         greet(row, col_of(k))
-    for k in range(cols):
-        greet(chip * 2 + 1 - core, col_of(k))
+        greet(at_row(1, 0, 0), col_of(k))
+    for k in range(ring):
+        greet(at_row(0, k, 1), me)
 
     small = [
         pltpu.make_async_copy(a, b, semI.at[n])
@@ -101,8 +106,6 @@
     same = (i0 // BINS) == ((i1 % 128) // BINS)
     sums[...] = jnp.where(same & ((i0 <= i1) | (i1 >= 128)), 1.0, 0.0)
 
-    aug[feats:, :] = jnp.where(lax.broadcasted_iota(jnp.int32, (16, samples), 0) == 0, 1.0, 0.0).astype(BF16)
-
     for copy in small[:2]:
         copy.wait()
 
@@ -118,12 +121,19 @@
 
     top = rows_of(lax.broadcasted_iota(jnp.int32, (SUB, 256), 0))
 
+    ones = jnp.where(lax.broadcasted_iota(jnp.int32, (16, C), 0) == 0, 1.0, 0.0).astype(BF16)
+
+    def cast(n, _):
+        where = pl.ds(pl.multiple_of(n * C, C), C)
+        aug[0:feats, where] = codes_ref[:, where].astype(BF16)
+        aug[feats:, where] = ones
+        return 0
+
     for q in range(PARTS):
-        at = slice(q * Kc, (q + 1) * Kc)
         big[q].wait()
-        aug[0:feats, at] = codes_ref[:, at].astype(BF16)
-
-    pl.semaphore_wait(barrier, (cols - 1) + cols + (chips - 1))
+        lax.fori_loop(q * cols, (q + 1) * cols, cast, 0)
+
+    pl.semaphore_wait(barrier, (chips - 1) + 2 * (cols - 1) + ring)
 
     def to_col(src, dst, sent, came, k):
         return pltpu.make_async_remote_copy(
@@ -136,11 +146,22 @@
         t = jnp.dot(top, aug[:, chunk(q, c)], preferred_element_type=F32)
         return jnp.where(t > 0.0, 1.0, 0.0).astype(BF16)
 
-    for q in range(PARTS):
-        for k in range(1, cols):
-            sA[q, k] = top_bits(q, col_of(k))
+    def stepA(n, _):
+        q, k = n // cols, lax.rem(n, cols)
+        bits = top_bits(q, col_of(k))
+
+        @pl.when(k > 0)
+        def _():
+            sA[q, k] = bits
             to_col(sA.at[q, k], rA.at[q, k], semA.at[0, q], semA.at[1, q], k).start()
-        rA[q, 0] = top_bits(q, me)
+
+        @pl.when(k == 0)
+        def _():
+            rA[q, 0] = bits
+
+        return 0
+
+    lax.fori_loop(0, PARTS * cols, stepA, 0)
 
     at = lax.broadcasted_iota(jnp.int32, (256, 256), 0)
     t, r = at // SUB, at % SUB
@@ -160,13 +181,14 @@
             s = s + ref[q, k].astype(F32)
         return s
 
-    mine = []
-    for q in range(PARTS):
+    def stepS(q, _):
         wait_bytes(rA.at[q, others], semA.at[1, q])
-        mine.append(walk(total(rA, q)) - SUB)
-        subs[q, 0] = mine[q].astype(F32)
+        subs[q, 0] = (walk(total(rA, q)) - SUB).astype(F32)
         for k in range(1, cols):
             to_col(subs.at[q, 0], subs.at[q, k], sentS.at[q], semS.at[q, k], k).start()
+        return 0
+
+    lax.fori_loop(0, PARTS, stepS, 0)
 
     def deep_bits(q, c, sub):
         sub = jnp.broadcast_to(sub, (SUB, C)).astype(BF16)
@@ -175,17 +197,28 @@
             got = got + jnp.where(sub == BF16(t), tab[t * SUB : (t + 1) * SUB, chunk(q, c)], BF16(0))
         return jnp.where(got.astype(F32) > 0.0, 1.0, 0.0).astype(BF16)
 
-    for q in range(PARTS):
-        rB[q, 0] = deep_bits(q, me, mine[q].astype(F32))
-
-        def stepB(k, _):
+    def stepB(n, _):
+        q, k = n // cols, lax.rem(n, cols)
+        back = lax.rem(cols - k, cols)
+
+        @pl.when(k > 0)
+        def _():
             wait_bytes(subs.at[q, k], semS.at[q, k])
-            back = cols - k
-            sB[q, back] = deep_bits(q, col_of(back), subs[q, k])
+
+        bits = deep_bits(q, col_of(back), subs[q, k])
+
+        @pl.when(k > 0)
+        def _():
+            sB[q, back] = bits
             to_col(sB.at[q, back], rB.at[q, back], semB.at[0, q], semB.at[1, q], back).start()
-            return 0
-
-        lax.fori_loop(1, cols, stepB, 0)
+
+        @pl.when(k == 0)
+        def _():
+            rB[q, 0] = bits
+
+        return 0
+
+    lax.fori_loop(0, PARTS * cols, stepB, 0)
 
     for copy in small[2:]:
         copy.wait()
@@ -196,19 +229,27 @@
     r16 = lax.broadcasted_iota(jnp.int32, (16, 256), 0)
     leaves = jnp.where(r16 == 0, high, jnp.where(r16 == 1, mid, jnp.where(r16 == 2, rest, 0.0))).astype(BF16)
 
-    v8 = codes_ref[...].astype(I8)
-    for g in range(chips):
-        cs[g] = v8[GROUP * g : GROUP * (g + 1)]
-
-    for q in range(PARTS):
+    def narrow(n, _):
+        where = pl.ds(pl.multiple_of(n * C, C), C)
+        v8 = codes_ref[:, where].astype(I8)
+        for g in range(chips):
+            cs[g, :, where] = v8[GROUP * g : GROUP * (g + 1)]
+        return 0
+
+    lax.fori_loop(0, PARTS * cols, narrow, 0)
+
+    def stepP(q, _):
         wait_bytes(rB.at[q, others], semB.at[1, q])
-        slot = mine[q] * 16 + walk(total(rB, q)) - SUB
+        slot = subs[q, 0].astype(jnp.int32) * 16 + walk(total(rB, q)) - SUB
         onehot = jnp.where(lax.broadcasted_iota(jnp.int32, (256, C), 0) == slot, 1.0, 0.0).astype(BF16)
         parts = jnp.dot(leaves, onehot, preferred_element_type=F32)
         weight = parts[0:1] + parts[1:2] + parts[2:3]
         ps[q, 0] = jax.nn.sigmoid(base_ref[q * cols + me] + weight)
         for k in range(1, cols):
             to_col(ps.at[q, 0], ps.at[q, k], sentP.at[q], semP.at[q, k], k).start()
+        return 0
+
+    lax.fori_loop(0, PARTS, stepP, 0)
 
     def weights(q, k, c):
         p = ps[q, k]
@@ -223,15 +264,17 @@
             both = jnp.concatenate([jnp.where(node, a, BF16(0)), jnp.where(node, b, BF16(0))], axis=0)
             W[i * 32 : (i + 1) * 32, chunk(q, c)] = both.astype(F8)
 
-    def all_weights(q):
-        weights(q, 0, me)
-
-        def stepW(k, _):
+    def stepW(n, _):
+        q, k = n // cols, lax.rem(n, cols)
+
+        @pl.when(k > 0)
+        def _():
             wait_bytes(ps.at[q, k], semP.at[q, k])
-            weights(q, k, col_of(cols - k))
-            return 0
-
-        lax.fori_loop(1, cols, stepW, 0)
+
+        weights(q, k, col_of(lax.rem(cols - k, cols)))
+        return 0
+
+    lax.fori_loop(0, PARTS * cols, stepW, 0)
 
     def chip_of(i):
         j, far = lax.rem(i, ring), 1 - i // ring
@@ -251,51 +294,49 @@
             device_id=(chip_of(i) * 2 + core, me), device_id_type=MESH,
         )
 
-    for q in range(PARTS):
-        all_weights(q)
-
     bins = lax.broadcasted_iota(jnp.int32, (BINS, samples), 0).astype(I8)
 
-    def block(i):
-        g = chip_of(i)
+    def blocks(n):
         onehot = jnp.concatenate(
             [
                 jnp.where(
                     jnp.broadcast_to(cs[g, f : f + 1, :], (BINS, samples)) == bins, jnp.ones((), F8), jnp.zeros((), F8)
                 )
+                for g in (chip_of(2 * n), chip_of(2 * n + 1))
                 for f in range(GROUP)
             ],
             axis=0,
         )
         acc = lax.dot_general(W[...], onehot, (((1,), (1,)), ((), ())), preferred_element_type=F32)
         out = acc[0:32] * PIECE_SCALES[0]
-        for n in range(1, PIECES):
-            out = out + acc[n * 32 : (n + 1) * 32] * PIECE_SCALES[n]
+        for p in range(1, PIECES):
+            out = out + acc[p * 32 : (p + 1) * 32] * PIECE_SCALES[p]
         out = jnp.concatenate([out[0:16], out[16:32] * 0.25], axis=0)
-        left, right = out[:, 0:128], out[:, 128:256]
         first = core == 0
-        hs[i] = jnp.where(first, left, right)
-        pair_s[i] = jnp.where(first, right, left)
-        pair(i).start()
+        for h in range(2):
+            left, right = out[:, 256 * h : 256 * h + 128], out[:, 256 * h + 128 : 256 * h + 256]
+            hs[2 * n + h] = jnp.where(first, left, right)
+            pair_s[2 * n + h] = jnp.where(first, right, left)
+            pair(2 * n + h).start()
 
     def merge(i):
         wait_bytes(pair_r.at[i], semX.at[i])
         hs[i] = hs[i] + pair_r[i]
 
     def stepH(n, _):
-        block(2 * n)
+        blocks(n)
 
         @pl.when(n > 0)
         def _():
-            merge(2 * n - 1)
-            share(2 * n - 1).start()
-
-        block(2 * n + 1)
-        merge(2 * n)
-        share(2 * n).start()
+            for i in (2 * n - 2, 2 * n - 1):
+                merge(i)
+                share(i).start()
+
         return 0
 
     lax.fori_loop(0, chips // 2, stepH, 0)
+    merge(chips - 2)
+    share(chips - 2).start()
     merge(chips - 1)
     wait_bytes(hr.at[pl.ds(0, chips - 1)], semH.at[1])
     hist = hs[chips - 1]
@@ -329,10 +370,8 @@
             best = jnp.maximum(best, got[k])
         return best
 
-    best = exchange(chips, m1s, m1r, semM, lambda k: (lax.rem(chip + k, chips) * 2 + core, me), best)
-    best = exchange(
-        2 * cols, m2s, m2r, semN, lambda k: (chip * 2 + lax.rem(core + k // cols, 2), col_of(k % cols)), best
-    )
+    best = exchange(2 * ring, m1s, m1r, semM, lambda k: (at_row(0, k % ring, k // ring), me), best)
+    best = exchange(planes * cols, m2s, m2r, semN, lambda k: (at_row(k // cols, 0, 0), col_of(k % cols)), best)
     out_ref[NODES:, :] = jnp.broadcast_to(best, (8, 128))
 
     for q in range(PARTS):
@@ -342,8 +381,13 @@
         wait_bytes(ps.at[q, others], sentP.at[q])
     wait_bytes(pair_s, sentX.at[0])
     wait_bytes(hs.at[pl.ds(0, chips - 1)], semH.at[0])
-    wait_bytes(m1r.at[pl.ds(1, chips - 1)], semM.at[0])
-    wait_bytes(m2r.at[pl.ds(1, 2 * cols - 1)], semN.at[0])
+    wait_bytes(m1r.at[pl.ds(1, 2 * ring - 1)], semM.at[0])
+    wait_bytes(m2r.at[pl.ds(1, planes * cols - 1)], semN.at[0])
+
+
+def finish(both_ref, gains_ref, best_ref):
+    gains_ref[...] = both_ref[0:NODES]
+    best_ref[...] = both_ref[NODES : NODES + 1, 0:NODES]
 
 
 def shards(cols, rows, codes, labels, base_margin, node_id, split_feature, threshold, leaf_value):
@@ -411,7 +455,13 @@
         codes, by_chunk(labels), by_chunk(base_margin), by_chunk(node_id),
         split_feature.reshape(1, 256), threshold.reshape(1, 256), leaf_value.reshape(1, 256),
     )
-    return out[0:NODES], out[NODES, 0:NODES]
+    gains, best = pl.pallas_call(
+        finish,
+        out_shape=(jax.ShapeDtypeStruct((NODES, 128), F32), jax.ShapeDtypeStruct((1, NODES), F32)),
+        in_specs=[vm],
+        out_specs=(vm, vm),
+    )(out)
+    return gains, best.reshape(NODES)
 
 
 def solution(mesh):

time: 77.3 us -> 62.5 us (0.81)
  Pallas kernels: 74 us -> 61.7 us
  local copies, waits for them, and re-layouts: 2.48 us -> 0 us
    pallas_call x1, Pallas kernels: 74 us -> 60.4 us  [shards(): pl.pallas_call(functools.partial(kernel, cols, chips), out_shape=jax.Shap...]
    pallas_call x0 -> x1, Pallas kernels: none -> 1.31 us  [shards(): pl.pallas_call(finish, out_shape=(jax.ShapeDtypeStruct((NODES, 128), F32)...]
    slice x1 -> x0, local copies, waits for them, and re-layouts: 1.29 us -> none  [shards(): return (out[0:NODES], out[NODES, 0:NODES])]
    squeeze x1 -> x0, local copies, waits for them, and re-layouts: 1.19 us -> none  [shards(): return (out[0:NODES], out[NODES, 0:NODES])]
where the time goes in v4:
time: 62.5 us; the launch traced here: 62.3 us
  Pallas kernels  61.7 us (99%)
  between operations  0.64 us (1%)
    pallas_call x1, Pallas kernels, shards(): pl.pallas_call(functools.partial(kernel, cols, chips), out_shape=jax.Shap...  60.4 us
    pallas_call x1, Pallas kernels, shards(): pl.pallas_call(finish, out_shape=(jax.ShapeDtypeStruct((NODES, 128), F32)...  1.31 us

profile of v4, /device:TPU:1, one launch (start us, length us, event | category | flops | bytes accessed | tf_op | source)
XLA Modules:
  0.0 62.3 jit_solution(16617594881414998860)
XLA Ops:
  0.6 60.4 %shard_map.86.both_ref = f32[24,128]{1,0:T(8,128)} custom-call(s32[64,12288]{1,0:T(8,128)} %codes_in.1, s32[16,1,768]{2,1,0:T(1,128)} %bitcast.7, f32[16,1,768]{2,1,0:T(1,128)} %bitcast.8, s32[16,1,768]{2,1,0:T(1,128)} %bitcast.9, s32[1,256]{1,0:T(1,128)} %bitcast.10, s32[1,256]{1,0:T(1,128)} %bitcast.11, f32[1,256]{1,0:T(1,128)} %bitcast.12), custom_call_target="tpu_custom_call" | custom-call | flops 25769803776 | bytes 3145728 | tf_op jit(solution)/shard_map/pallas_call | solution.py:402
  61.0 1.3 %shard_map.87 = (f32[16,128]{1,0:T(8,128)}, f32[1,16]{1,0:T(1,128)}) custom-call(f32[24,128]{1,0:T(8,128)} %shard_map.86.both_ref), custom_call_target="tpu_custom_call" | custom-call | tf_op jit(solution)/shard_map/pallas_call | solution.py:458

commit v5 on v4

--- a/solution.py
+++ b/solution.py
@@ -75,6 +75,19 @@
     def chunk(q, c):
         return pl.ds(pl.multiple_of((q * cols + c) * C, C), C)
 
+    small = [
+        pltpu.make_async_copy(a, b, semI.at[n])
+        for n, (a, b) in enumerate(
+            [(sf_in, sf_ref), (thr_in, thr_ref), (leaf_in, leaf_ref), (base_in, base_ref), (labels_in, labels_ref), (node_in, node_ref)]
+        )
+    ]
+    big = []
+    for q in range(PARTS):
+        at = pl.ds(q * Kc, Kc)
+        big.append(pltpu.make_async_copy(codes_in.at[:, at], codes_ref.at[:, at], semC.at[q]))
+    for copy in small[:2] + big + small[2:]:
+        copy.start()
+
     barrier = pltpu.get_barrier_semaphore()
 
     def greet(r, c):
@@ -88,23 +101,10 @@
     for k in range(ring):
         greet(at_row(0, k, 1), me)
 
-    small = [
-        pltpu.make_async_copy(a, b, semI.at[n])
-        for n, (a, b) in enumerate(
-            [(sf_in, sf_ref), (thr_in, thr_ref), (leaf_in, leaf_ref), (base_in, base_ref), (labels_in, labels_ref), (node_in, node_ref)]
-        )
-    ]
-    big = []
-    for q in range(PARTS):
-        at = pl.ds(q * Kc, Kc)
-        big.append(pltpu.make_async_copy(codes_in.at[:, at], codes_ref.at[:, at], semC.at[q]))
-    for copy in small[:2] + big + small[2:]:
-        copy.start()
-
     i0 = lax.broadcasted_iota(jnp.int32, (128, 256), 0)
     i1 = lax.broadcasted_iota(jnp.int32, (128, 256), 1)
     same = (i0 // BINS) == ((i1 % 128) // BINS)
-    sums[...] = jnp.where(same & ((i0 <= i1) | (i1 >= 128)), 1.0, 0.0)
+    sums[...] = jnp.where(same & ((i0 <= i1) | (i1 >= 128)), 1.0, 0.0).astype(BF16)
 
     for copy in small[:2]:
         copy.wait()
@@ -317,7 +317,19 @@
             left, right = out[:, 256 * h : 256 * h + 128], out[:, 256 * h + 128 : 256 * h + 256]
             hs[2 * n + h] = jnp.where(first, left, right)
             pair_s[2 * n + h] = jnp.where(first, right, left)
-            pair(2 * n + h).start()
+
+        @pl.when(n < chips // 2 - 1)
+        def _():
+            pair(2 * n).start()
+
+        pair(2 * n + 1).start()
+
+
+    def across():
+        return pltpu.make_async_remote_copy(
+            src_ref=pair_s.at[chips - 2], dst_ref=hr.at[chips - 1], send_sem=semH.at[0], recv_sem=semH.at[1],
+            device_id=(chip_of(chips - 2) * 2 + 1 - core, me), device_id_type=MESH,
+        )
 
     def merge(i):
         wait_bytes(pair_r.at[i], semX.at[i])
@@ -326,6 +338,11 @@
     def stepH(n, _):
         blocks(n)
 
+        @pl.when(n == chips // 2 - 1)
+        def _():
+            share(chips - 2).start()
+            across().start()
+
         @pl.when(n > 0)
         def _():
             for i in (2 * n - 2, 2 * n - 1):
@@ -335,15 +352,17 @@
         return 0
 
     lax.fori_loop(0, chips // 2, stepH, 0)
-    merge(chips - 2)
-    share(chips - 2).start()
     merge(chips - 1)
-    wait_bytes(hr.at[pl.ds(0, chips - 1)], semH.at[1])
+    wait_bytes(hr, semH.at[1])
     hist = hs[chips - 1]
-    for i in range(chips - 1):
+    for i in range(chips):
         hist = hist + hr[i]
 
-    both = jnp.dot(hist, sums[...], precision=lax.Precision.HIGHEST, preferred_element_type=F32)
+    high = hist.astype(BF16).astype(F32)
+    mid = (hist - high).astype(BF16).astype(F32)
+    three = jnp.concatenate([high, mid, hist - high - mid], axis=0).astype(BF16)
+    three = jnp.dot(three, sums[...], preferred_element_type=F32)
+    both = three[0:32] + (three[32:64] + three[64:96])
     left, node = both[:, 0:128], both[:, 128:256]
     right = node - left
 
@@ -379,8 +398,8 @@
         wait_bytes(sB.at[q, others], semB.at[0, q])
         wait_bytes(subs.at[q, others], sentS.at[q])
         wait_bytes(ps.at[q, others], sentP.at[q])
-    wait_bytes(pair_s, sentX.at[0])
-    wait_bytes(hs.at[pl.ds(0, chips - 1)], semH.at[0])
+    wait_bytes(pair_s.at[pl.ds(0, chips - 1)], sentX.at[0])
+    wait_bytes(hs, semH.at[0])
     wait_bytes(m1r.at[pl.ds(1, 2 * ring - 1)], semM.at[0])
     wait_bytes(m2r.at[pl.ds(1, planes * cols - 1)], semN.at[0])
 
@@ -412,7 +431,7 @@
             pltpu.VMEM((1, 256), I32),
             pltpu.VMEM((1, 256), I32),
             pltpu.VMEM((1, 256), F32),
-            pltpu.VMEM((128, 256), F32),
+            pltpu.VMEM((128, 256), BF16),
             pltpu.VMEM((feats + 16, samples), BF16),
             pltpu.VMEM((chips, GROUP, samples), I8),
             pltpu.VMEM((256, samples), BF16),

time: 62.5 us -> 62.6 us (level)
  no operation moved by 1% of the time
where the time goes in v5:
time: 62.6 us; the launch traced here: 62.4 us
  Pallas kernels  61.8 us (99%)
  between operations  0.64 us (1%)
    pallas_call x1, Pallas kernels, shards(): pl.pallas_call(functools.partial(kernel, cols, chips), out_shape=jax.Shap...  60.5 us
    pallas_call x1, Pallas kernels, shards(): pl.pallas_call(finish, out_shape=(jax.ShapeDtypeStruct((NODES, 128), F32)...  1.31 us

profile of v5, /device:TPU:1, one launch (start us, length us, event | category | flops | bytes accessed | tf_op | source)
XLA Modules:
  0.0 62.4 jit_solution(9765816578666346995)
XLA Ops:
  0.6 60.5 %shard_map.86.both_ref = f32[24,128]{1,0:T(8,128)} custom-call(s32[64,12288]{1,0:T(8,128)} %codes_in.1, s32[16,1,768]{2,1,0:T(1,128)} %bitcast.7, f32[16,1,768]{2,1,0:T(1,128)} %bitcast.8, s32[16,1,768]{2,1,0:T(1,128)} %bitcast.9, s32[1,256]{1,0:T(1,128)} %bitcast.10, s32[1,256]{1,0:T(1,128)} %bitcast.11, f32[1,256]{1,0:T(1,128)} %bitcast.12), custom_call_target="tpu_custom_call" | custom-call | flops 25769803776 | bytes 3145728 | tf_op jit(solution)/shard_map/pallas_call | solution.py:421
  61.1 1.3 %shard_map.87 = (f32[16,128]{1,0:T(8,128)}, f32[1,16]{1,0:T(1,128)}) custom-call(f32[24,128]{1,0:T(8,128)} %shard_map.86.both_ref), custom_call_target="tpu_custom_call" | custom-call | tf_op jit(solution)/shard_map/pallas_call | solution.py:477

commit v6 on v5

--- a/solution.py
+++ b/solution.py
@@ -296,33 +296,35 @@
 
     bins = lax.broadcasted_iota(jnp.int32, (BINS, samples), 0).astype(I8)
 
-    def blocks(n):
+    def block(i):
+        g = chip_of(i)
         onehot = jnp.concatenate(
             [
                 jnp.where(
                     jnp.broadcast_to(cs[g, f : f + 1, :], (BINS, samples)) == bins, jnp.ones((), F8), jnp.zeros((), F8)
                 )
-                for g in (chip_of(2 * n), chip_of(2 * n + 1))
                 for f in range(GROUP)
             ],
             axis=0,
         )
         acc = lax.dot_general(W[...], onehot, (((1,), (1,)), ((), ())), preferred_element_type=F32)
         out = acc[0:32] * PIECE_SCALES[0]
-        for p in range(1, PIECES):
-            out = out + acc[p * 32 : (p + 1) * 32] * PIECE_SCALES[p]
+        for n in range(1, PIECES):
+            out = out + acc[n * 32 : (n + 1) * 32] * PIECE_SCALES[n]
         out = jnp.concatenate([out[0:16], out[16:32] * 0.25], axis=0)
+        left, right = out[:, 0:128], out[:, 128:256]
         first = core == 0
-        for h in range(2):
-            left, right = out[:, 256 * h : 256 * h + 128], out[:, 256 * h + 128 : 256 * h + 256]
-            hs[2 * n + h] = jnp.where(first, left, right)
-            pair_s[2 * n + h] = jnp.where(first, right, left)
-
-        @pl.when(n < chips // 2 - 1)
-        def _():
-            pair(2 * n).start()
-
-        pair(2 * n + 1).start()
+        hs[i] = jnp.where(first, left, right)
+        pair_s[i] = jnp.where(first, right, left)
+
+        @pl.when(i != chips - 2)
+        def _():
+            pair(i).start()
+
+        @pl.when(i == chips - 2)
+        def _():
+            share(i).start()
+            across().start()
 
 
     def across():
@@ -335,23 +337,17 @@
         wait_bytes(pair_r.at[i], semX.at[i])
         hs[i] = hs[i] + pair_r[i]
 
-    def stepH(n, _):
-        blocks(n)
-
-        @pl.when(n == chips // 2 - 1)
-        def _():
-            share(chips - 2).start()
-            across().start()
-
-        @pl.when(n > 0)
-        def _():
-            for i in (2 * n - 2, 2 * n - 1):
-                merge(i)
-                share(i).start()
-
-        return 0
-
-    lax.fori_loop(0, chips // 2, stepH, 0)
+    def stepH(i, _):
+        block(i)
+
+        @pl.when((i > 0) & (i < chips - 1))
+        def _():
+            merge(i - 1)
+            share(i - 1).start()
+
+        return 0
+
+    lax.fori_loop(0, chips, stepH, 0)
     merge(chips - 1)
     wait_bytes(hr, semH.at[1])
     hist = hs[chips - 1]

time: 62.6 us -> 62.9 us (level)
  no operation moved by 1% of the time
where the time goes in v6:
time: 62.9 us; the launch traced here: 62.7 us
  Pallas kernels  62.1 us (99%)
  between operations  0.64 us (1%)
    pallas_call x1, Pallas kernels, shards(): pl.pallas_call(functools.partial(kernel, cols, chips), out_shape=jax.Shap...  60.8 us
    pallas_call x1, Pallas kernels, shards(): pl.pallas_call(finish, out_shape=(jax.ShapeDtypeStruct((NODES, 128), F32)...  1.31 us

profile of v6, /device:TPU:1, one launch (start us, length us, event | category | flops | bytes accessed | tf_op | source)
XLA Modules:
  0.0 62.7 jit_solution(17119258132605814188)
XLA Ops:
  0.6 60.8 %shard_map.86.both_ref = f32[24,128]{1,0:T(8,128)} custom-call(s32[64,12288]{1,0:T(8,128)} %codes_in.1, s32[16,1,768]{2,1,0:T(1,128)} %bitcast.7, f32[16,1,768]{2,1,0:T(1,128)} %bitcast.8, s32[16,1,768]{2,1,0:T(1,128)} %bitcast.9, s32[1,256]{1,0:T(1,128)} %bitcast.10, s32[1,256]{1,0:T(1,128)} %bitcast.11, f32[1,256]{1,0:T(1,128)} %bitcast.12), custom_call_target="tpu_custom_call" | custom-call | flops 25769803776 | bytes 3145728 | tf_op jit(solution)/shard_map/pallas_call | solution.py:417
  61.4 1.3 %shard_map.87 = (f32[16,128]{1,0:T(8,128)}, f32[1,16]{1,0:T(1,128)}) custom-call(f32[24,128]{1,0:T(8,128)} %shard_map.86.both_ref), custom_call_target="tpu_custom_call" | custom-call | tf_op jit(solution)/shard_map/pallas_call | solution.py:473
